TPU v7x, 32 devices: a whole 2x2x4 slice. The times are simulated.
32 devices in a mesh: segment: 16 (over z, x, core), band: 2 (over y).
Axes of the slice: x: 2, y: 2, z: 4, core: 2. Of those that a mesh axis runs over, the one named last changes fastest.
Arguments:
- first_input: bfloat16 [16, 16, 128, 256], P('segment', 'band'), may hold values from -6 to 6
- stashed: bfloat16 [16, 2, 16, 128, 256], P('segment', None, 'band'), may hold values from -6 to 6
- first_grad: bfloat16 [16, 16, 128, 256], P('segment', 'band'), may hold values from -6 to 6
- weight_now: bfloat16 [16, 3, 3, 256, 256], P('segment'), may hold values from -5 to 5
- weight_old: bfloat16 [16, 3, 3, 256, 256], P('segment'), may hold values from -5 to 5
- momentum: float32 [16, 3, 3, 256, 256], P('segment'), may hold values from -6 to 6
- slot_plan: int32 [2, 16], P(None, 'segment'), may hold values from 0 to 1
- next_input: bfloat16 [16, 128, 256], P('band'), may hold values from -6 to 6
- next_grad: bfloat16 [16, 128, 256], P('band'), may hold values from -6 to 6
Outputs:
- act_out: bfloat16 [16, 16, 128, 256], P('segment', 'band')
- grad_out: bfloat16 [16, 16, 128, 256], P('segment', 'band')
- weight_now_out: bfloat16 [16, 3, 3, 256, 256], P('segment')
- weight_old_out: bfloat16 [16, 3, 3, 256, 256], P('segment')
- momentum_out: float32 [16, 3, 3, 256, 256], P('segment')
All inputs are finite; a program needn't handle non-finite values.
Results may differ from a plain program's by a relative error of at most 0.009.
Values may be sent and summed in bfloat16 or wider, within the bound.
No kernel may reach another device: no remote copies, remote signals or barrier semaphores. Data moves between devices by JAX's collectives and lax.ppermute only.
A program may use at most 128 MiB of HBM per device.

v0:
```python
import functools
import math

import jax
import jax.numpy as jnp
from jax import lax
from jax.experimental import pallas as pl
from jax.experimental.pallas import tpu as pltpu
from jax.sharding import PartitionSpec as P

C = 256


def padded_2(block, sides, width):
    for axis, dim in sides:
        count = lax.axis_size(axis)
        forward = [(i, i + 1) for i in range(count - 1)]
        backward = [(target, source) for source, target in forward]
        low = lax.ppermute(
            lax.slice_in_dim(block, block.shape[dim] - width, None, axis=dim), axis, forward
        )
        high = lax.ppermute(lax.slice_in_dim(block, 0, width, axis=dim), axis, backward)
        block = jnp.concatenate([low, block, high], axis=dim)
    return block


def passed_along(array, axis, by):
    length = lax.axis_size(axis)
    pairs = [(i, i + by) for i in range(length) if 0 <= i + by < length]
    return lax.ppermute(array, axis, pairs)


def row_patches(extended, rows):
    wcol = extended.shape[1]
    padded = jnp.pad(extended, ((0, 0), (1, 1), (0, 0)))
    taps = [padded[ky : ky + rows, kx : kx + wcol, :] for ky in range(3) for kx in range(3)]
    return jnp.concatenate(taps, axis=2).reshape(rows * wcol, -1)


def silu_slope(value):
    sig = jax.nn.sigmoid(value)
    return sig * (1.0 + value * (1.0 - sig))


def forward_part(x_in, flat_now, factor):
    rows, wcol = (x_in.shape[0], x_in.shape[1])
    ext = padded_2(x_in, (("band", 0),), 1)
    pre = jnp.dot(row_patches(ext, rows), flat_now, preferred_element_type=jnp.float32) * factor
    return jax.nn.silu(pre).astype(jnp.bfloat16).reshape(rows, wcol, C)


def backward_part(chosen, grad, w_old, factor):
    rows, wcol = (chosen.shape[0], chosen.shape[1])
    flat_old = w_old.reshape(9 * C, C)
    flip_old = w_old[::-1, ::-1].transpose(0, 1, 3, 2).reshape(9 * C, C)
    ext = padded_2(chosen, (("band", 0),), 1)
    patches = row_patches(ext, rows)
    back = jnp.dot(patches, flat_old, preferred_element_type=jnp.float32) * factor
    slope_grad = (grad.reshape(-1, C) * silu_slope(back)).astype(jnp.bfloat16)
    slope_ext = padded_2(slope_grad.reshape(rows, wcol, C), (("band", 0),), 1)
    kgrad = (
        lax.dot_general(
            patches, slope_grad, (((0,), (0,)), ((), ())), preferred_element_type=jnp.float32
        )
        * factor
    )
    in_grad = (
        jnp.dot(row_patches(slope_ext, rows), flip_old, preferred_element_type=jnp.float32) * factor
    )
    return (in_grad.astype(jnp.bfloat16).reshape(rows, wcol, C), kgrad)


def update_part(kgrad, w_now, moment):
    flat_now = w_now.reshape(9 * C, C).astype(jnp.float32)
    total = lax.psum(kgrad.astype(jnp.bfloat16), "band").astype(jnp.float32)
    new_moment = 0.9 * moment + total
    new_flat = (flat_now - 0.05 * new_moment).astype(jnp.bfloat16)
    return (new_flat.reshape(3, 3, C, C), new_moment)


def body(
    first_input,
    stashed,
    first_grad,
    weight_now,
    weight_old,
    momentum,
    slot_plan,
    next_input,
    next_grad,
):
    factor = 1.0 / math.sqrt(9 * C)
    segment_pos = lax.axis_index("segment")
    last_pos = lax.axis_size("segment") - 1
    x_in = first_input[0]
    stash = stashed[0]
    grad = first_grad[0]
    w_now = weight_now[0]
    w_old = weight_old[0]
    moment = momentum[0].reshape(9 * C, C)
    slots = slot_plan[:, 0]
    for tick in range(2):
        if tick == 1:
            arrived = passed_along(out_acts, "segment", 1)
            x_in = jnp.where(segment_pos == 0, next_input, arrived)
            returned = passed_along(in_grad, "segment", -1)
            grad = jnp.where(segment_pos == last_pos, next_grad, returned)
        out_acts = forward_part(x_in, w_now.reshape(9 * C, C), factor)
        chosen = lax.dynamic_index_in_dim(stash, slots[tick], 0, keepdims=False)
        in_grad, kgrad = backward_part(chosen, grad, w_old, factor)
        stash = lax.dynamic_update_index_in_dim(stash, x_in, slots[tick], 0)
        new_weight, moment = update_part(kgrad, w_now, moment)
        w_old = w_now
        w_now = new_weight
    return (out_acts[None], in_grad[None], w_now[None], w_old[None], moment.reshape(1, 3, 3, C, C))


SWAP = [(0, 1), (1, 0)]
BF16 = jnp.bfloat16
F32 = jnp.float32
NT = (((1,), (1,)), ((), ()))
TN = (((0,), (0,)), ((), ()))
MIB = 2**20


def vmem(count):
    return [pl.BlockSpec(memory_space=pltpu.VMEM)] * count


def anywhere(count):
    return [pl.BlockSpec(memory_space=pl.ANY)] * count


def hbm(count):
    return [pl.BlockSpec(memory_space=pltpu.HBM)] * count


SMEM = pl.BlockSpec(memory_space=pltpu.SMEM)


def call(kernel, outs, in_specs, out_specs, scratch, limit=24):
    count = len(in_specs)

    def ordered(*refs):
        kernel(lax.axis_index("band"), *refs[:count], *refs[count + 1 :])

    return pl.pallas_call(
        ordered,
        name=kernel.__name__,
        out_shape=[jax.ShapeDtypeStruct(shape, kind) for shape, kind in outs],
        in_specs=in_specs + anywhere(1),
        out_specs=out_specs,
        scratch_shapes=scratch,
        compiler_params=pltpu.CompilerParams(vmem_limit_bytes=limit * MIB),
        cost_estimate=pl.CostEstimate(flops=10**10, bytes_accessed=10**8, transcendentals=0),
    )


def conv_rows(rows_of, start, count, taps):
    lhs = [rows_of[pl.ds(start + ky, count)] for ky in range(3)]
    wcol = lhs[0].shape[1]
    lhs = jnp.concatenate([part.reshape(count * wcol, C) for part in lhs], axis=1)
    left, mid, right = (
        part.reshape(count, wcol, C) for part in (taps(lhs, 0), taps(lhs, 1), taps(lhs, 2))
    )
    col = lax.broadcasted_iota(jnp.int32, mid.shape, 1)
    left = jnp.where(col == 0, 0.0, pltpu.roll(left, 1, 1))
    right = jnp.where(col == wcol - 1, 0.0, pltpu.roll(right, wcol - 1, 1))
    return (left + mid + right) * (1.0 / math.sqrt(9 * C))


def on_either_side(me, part):
    for side in range(2):
        pl.when(me == side)(functools.partial(part, side))


def taps_of(kernel_ref):
    def taps(lhs, kx):
        rhs = jnp.concatenate([kernel_ref[0, ky, kx] for ky in range(3)], axis=0)
        return jnp.dot(lhs, rhs, preferred_element_type=F32)

    return taps


def flipped_taps_of(kernel_ref):
    def taps(lhs, kx):
        rhs = jnp.concatenate([kernel_ref[0, 2 - ky, 2 - kx] for ky in range(3)], axis=1)
        return lax.dot_general(lhs, rhs, NT, preferred_element_type=F32)

    return taps


def chunks(count):
    return [(at, min(2, count - at)) for at in range(0, count, 2)]


def silu_rows(maps, kernel_ref, count, out_ref, base=0):
    for at, size in chunks(count):
        pre = conv_rows(maps, base + at, size, taps_of(kernel_ref))
        out_ref[pl.ds(base + at, size)] = (pre / (1.0 + jnp.exp(-pre))).astype(BF16)


def slope_rows(maps, start, kernel_ref, count, store):
    for at, size in chunks(count):
        back = conv_rows(maps, start + at, size, taps_of(kernel_ref))
        sig = 1.0 / (1.0 + jnp.exp(-back))
        store(at, sig * (1.0 + back * (1.0 - sig)))


def put_dz(dz3, to, dz):
    wcol = dz.shape[1]
    col = lax.broadcasted_iota(jnp.int32, dz.shape, 1)
    row = pl.ds(to, dz.shape[0])
    dz3[row, :, 0:C] = jnp.where(col == 0, 0.0, pltpu.roll(dz, 1, 1)).astype(BF16)
    dz3[row, :, C : 2 * C] = dz.astype(BF16)
    dz3[row, :, 2 * C :] = jnp.where(
        col == wcol - 1, 0.0, pltpu.roll(dz, wcol - 1, 1)
    ).astype(BF16)


def dz_from(maps, start, kernel_ref, grads, grads_at, count, dz3, to):
    def job(at, size):
        def run():
            def store(_, slope):
                grad = grads[pl.ds(grads_at + at, size)].astype(F32)
                put_dz(dz3, to + at, grad * slope)

            slope_rows(maps, start + at, kernel_ref, size, store)

        return (to + at, size, run)

    return [job(at, size) for at, size in chunks(count)]


def dz_from_slopes(slopes, grads, grads_at, count, dz3, to):
    def job(at, size):
        def run():
            grad = grads[pl.ds(grads_at + at, size)].astype(F32)
            put_dz(dz3, to + at, grad * slopes[pl.ds(at, size)])

        return (to + at, size, run)

    return [job(at, size) for at, size in chunks(count)]


def dz_and_in_grad(jobs, there, dz3, kernel_ref, count, out_ref):
    there = set(there)
    waiting = chunks(count)
    for first, rows, run in jobs:
        run()
        there.update(range(first, first + rows))
        for at, size in list(waiting):
            if there.issuperset(range(at, at + size + 2)):
                dx = conv_rows(Middle(dz3), at, size, flipped_taps_of(kernel_ref))
                out_ref[pl.ds(at, size)] = dx.astype(BF16)
                waiting.remove((at, size))
    assert not waiting


class Middle:
    def __init__(self, dz3):
        self.dz3 = dz3

    def __getitem__(self, rows):
        return self.dz3[rows, :, C : 2 * C]


def kernel_grad(maps, start, dz3, dz_start, rows, ky):
    wcol = maps.shape[1]
    lhs = maps[pl.ds(start + ky, rows)].reshape(rows * wcol, C)
    rhs = dz3[pl.ds(dz_start, rows)].reshape(rows * wcol, 3 * C)
    grad = lax.dot_general(lhs, rhs, TN, preferred_element_type=F32) * (1.0 / math.sqrt(9 * C))
    return [grad[:, (2 - kx) * C : (3 - kx) * C] for kx in range(3)]


def zero_row(ref, at):
    ref[pl.ds(at, 1)] = jnp.zeros((1,) + ref.shape[1:], ref.dtype)


def put(ref, at, value):
    ref[pl.ds(at, value.shape[0])] = value


def put_second_map(ref, at, slots, x_in, stash):
    same = slots[0] == slots[1]

    @pl.when(same)
    def _():
        put(ref, at, x_in[0])

    @pl.when(jnp.logical_not(same))
    def _():
        put(ref, at, stash[0, slots[1]])


def edge(rows, count, me):
    return pl.ds((1 - me) * (rows - count), count)


def inner(rows, count, me):
    return pl.ds(me * (rows - count), count)


def start_copies(copies, sems, first):
    started = [
        pltpu.make_async_copy(a, b, sems.at[first + i]) for i, (a, b) in enumerate(copies)
    ]
    for copy in started:
        copy.start()
    return started


def pack(me, slots, x_in, stash, grad, edges, mark, sems):
    rows = stash.shape[2]
    mark[...] = jnp.zeros_like(mark)
    copies = start_copies(
        [
            (stash.at[0, slots[0], edge(rows, 3, me)], edges.at[pl.ds(0, 3)]),
            (grad.at[0, edge(rows, 2, me)], edges.at[pl.ds(3, 2)]),
            (x_in.at[0, edge(rows, 2, me)], edges.at[pl.ds(5, 2)]),
        ],
        sems, 0,
    )
    for copy in copies:
        copy.wait()


def pack_rest(
    me, slots, x_in, stash, grad, next_in, next_g, rest, one, two, next_kept, low, high
):
    rows = x_in.shape[1]
    one[...] = stash[0, slots[0]]
    put_second_map(two, 0, slots, x_in, stash)
    rest[0 : rows - 3] = one[inner(rows, rows - 3, me)]
    rest[rows - 3 :] = grad[0, inner(rows, rows - 2, me)]
    next_kept[...] = next_in[...]
    first = lax.axis_index("segment") == 0
    low[...] = next_g[0 : rows // 2]

    @pl.when(first)
    def _():
        high[...] = next_in[edge(rows, rows // 2, me)]

    @pl.when(jnp.logical_not(first))
    def _():
        high[...] = next_g[rows // 2 :]


def early(
    me, one, two, x_in, w_old, w_now, y1, slope1, slope2, edges2, maps_x, maps_one, maps_two,
):
    rows = x_in.shape[1]
    edges2[...] = two[edge(rows, 2, me)]
    for maps, source in ((maps_x, x_in[0]), (maps_one, one[...]), (maps_two, two[...])):
        zero_row(maps, rows * me)
        put(maps, 1 - me, source)

    def keep(slopes, base):
        def store(at, slope):
            slopes[pl.ds(base + at, slope.shape[0])] = slope

        return store

    def looped(step):
        pairs = (rows - 1) // 2
        lax.fori_loop(0, pairs, lambda at, _: step(2 * at, 2), None)
        if (rows - 1) % 2:
            step(2 * pairs, 1)

    looped(lambda at, size: slope_rows(maps_two, at, w_now, size, keep(slope2, at)))
    looped(lambda at, size: slope_rows(maps_one, at, w_old, size, keep(slope1, at)))
    looped(lambda at, size: silu_rows(maps_x, w_now, size, y1, at))


def forward_two(me, next_in, beside, arrived, w_one, act, maps):
    first = lax.axis_index("segment") == 0
    rows = next_in.shape[0]
    zero_row(maps, (rows + 1) * me)

    @pl.when(first)
    def _():
        put(maps, 1, next_in[...])
        put(maps, (rows + 1) * (1 - me), beside[pl.ds((rows // 2 - 1) * me, 1)])

    @pl.when(jnp.logical_not(first))
    def _():
        put(maps, 1 - me, arrived[...])

    silu_rows(maps, w_one, rows, act)


def backward_one(
    me, one, two, x_in, grad, edges, w_old, w_now, slope1, y1_far,
    dx, y1, rest2, dz3_edge, maps, dz3, border,
):
    rows = one.shape[0]
    rest2[...] = two[inner(rows, rows - 2, me)]
    put(border, 2 * me, x_in[0, edge(rows, 2, me)])
    put(border, 2 * (1 - me), edges[5:7])
    silu_rows(border, w_now, 2, y1.at[pl.ds((rows - 1) * (1 - me), 2)])
    put(y1, 2 * me, y1_far[...])
    zero_row(maps, (rows + 3) * me)
    put(maps, 1 + 2 * me, one[...])
    put(maps, (rows + 1) * (1 - me), edges[0:3])
    zero_row(dz3, (rows + 2) * me)

    def part(me):
        own = 1 + me
        near = own + (rows - 1) * (1 - me)
        other = own + rows * (1 - me) - 2 * me
        jobs = dz_from(maps, near - 1 + me, w_old, grad.at[0], (rows - 1) * (1 - me), 1, dz3, near)
        jobs += dz_from(maps, other - 1 + me, w_old, edges, 3, 2, dz3, other)
        jobs += dz_from_slopes(slope1, grad.at[0], me, rows - 1, dz3, own + me)
        dz_and_in_grad(jobs, [(rows + 2) * me], dz3, w_old, rows + 1, dx)

    on_either_side(me, part)
    dz3_edge[...] = dz3[pl.ds((rows + 1) * (1 - me), 2)]


def keep_kernel_grad(maps, start, dz3, dz_start, rows, out, unroll):
    def step(ky, _):
        taps = kernel_grad(maps, start, dz3, dz_start, rows, ky)
        for kx in range(3):
            out[ky, kx] = taps[kx]

    lax.fori_loop(0, 3, step, None, unroll=unroll)


def own_kernel_grad(me, maps, dz3, own_kgrad):
    rows = maps.shape[0] - 4
    keep_kernel_grad(maps, 2 * me, dz3, 1 + me, rows, own_kgrad, 1)


def backward_one_rest(
    me, one, edges, rest, dz3_edge, w_old, low, high, dx, maps, dz3, next_g_other
):
    rows = one.shape[0]
    zero_row(maps, (rows + 1) * (1 - me))
    put(next_g_other, 0, low[...])
    put(next_g_other, rows // 2, high[...])
    put(maps, (rows + 1) * me, one[edge(rows, 1, me)])
    put(maps, 1 + (rows - 3) * me, edges[0:3])
    put(maps, 4 - 3 * me, rest[0 : rows - 3])
    zero_row(dz3, rows * (1 - me))
    put(dz3, (rows - 1) * me, dz3_edge[...])

    def part(me):
        jobs = dz_from(maps, 2 * (1 - me), w_old, rest, rows - 3, rows - 2, dz3, 2 - me)
        there = [rows * (1 - me), (rows - 1) * me, (rows - 1) * me + 1]
        dz_and_in_grad(jobs, there, dz3, w_old, rows - 1, dx)

    on_either_side(me, part)


def update_one(me, maps, dz3, own_kgrad, moment, w_now, m_one, w_one):
    rows = maps.shape[0] - 2

    def step(ky, _):
        taps = kernel_grad(maps, 0, dz3, me, rows, ky)
        for kx in range(3):
            fresh = 0.9 * moment[0, ky, kx] + (own_kgrad[ky, kx] + taps[kx])
            m_one[ky, kx] = fresh
            w_one[0, ky, kx] = (w_now[0, ky, kx].astype(F32) - 0.05 * fresh).astype(BF16)

    lax.fori_loop(0, 3, step, None)


def backward_two(
    me, two, edges2, returned, next_g, next_g_other, w_now, slope2,
    dx, own_kgrad, dz3_edge, maps, grads, dz3,
):
    last = lax.axis_index("segment") == lax.axis_size("segment") - 1
    rows = two.shape[0]
    zero_row(maps, (rows + 2) * me)
    put(maps, 1 + me, two[...])
    put(maps, (rows + 1) * (1 - me), edges2[...])

    @pl.when(last)
    def _():
        put(grads, me, next_g[...])
        put(grads, rows * (1 - me), next_g_other[pl.ds((rows - 1) * me, 1)])

    @pl.when(jnp.logical_not(last))
    def _():
        put(grads, 0, returned[...])

    zero_row(dz3, (rows + 1) * me)

    def part(me):
        near = (rows - 1) * (1 - me)
        jobs = dz_from(maps, near, w_now, grads, near, 2, dz3, near + 1 - me)
        jobs += dz_from_slopes(slope2, grads, 2 * me, rows - 1, dz3, 1 + me)
        dz_and_in_grad(jobs, [(rows + 1) * me], dz3, w_now, rows, dx)

    on_either_side(me, part)
    dz3_edge[...] = dz3[pl.ds((rows + 1) * (1 - me), 1)]
    keep_kernel_grad(maps, me, dz3, 1, rows, own_kgrad, 3)


def finish(
    me, two, edges2, rest2, dz3_edge, returned, next_g_other, w_now,
    own_kgrad, m_one, w_one, dx, act,
    act_out, dx_out, m_out, w_out, w_one_out, maps, grads, dz3, m_two, w_two, sems,
):
    last = lax.axis_index("segment") == lax.axis_size("segment") - 1
    rows = two.shape[0]
    copies = start_copies(
        [(act, act_out.at[0]), (w_one, w_one_out), (dx, dx_out.at[0])], sems, 6
    )
    zero_row(maps, (rows + 1) * (1 - me))
    put(maps, (rows + 1) * me, two[edge(rows, 1, me)])
    put(maps, 1 + (rows - 2) * me, edges2[...])
    put(maps, 3 - 2 * me, rest2[...])

    @pl.when(last)
    def _():
        put(grads, 0, next_g_other[pl.ds(1 - me, rows - 1)])

    @pl.when(jnp.logical_not(last))
    def _():
        put(grads, 0, returned[...])

    put(dz3, (rows - 1) * me, dz3_edge[...])
    for _, _, run in dz_from(maps, 1 - me, w_now, grads, 0, rows - 1, dz3, 1 - me):
        run()

    def outputs(ky):
        return [(m_two.at[ky], m_out.at[0, ky]), (w_two.at[ky], w_out.at[0, ky])]

    def step(ky, _):
        taps = kernel_grad(maps, 0, dz3, 0, rows, ky)
        for kx in range(3):
            fresh = 0.9 * m_one[ky, kx] + (own_kgrad[ky, kx] + taps[kx])
            m_two[ky, kx] = fresh
            w_two[ky, kx] = (w_one[0, ky, kx].astype(F32) - 0.05 * fresh).astype(BF16)
        copies.extend(start_copies(outputs(ky), sems, 2 * ky))

    for ky in range(3):
        step(ky, None)
    for copy in copies:
        copy.wait()


def two_band_body(
    first_input, stashed, first_grad, weight_now, weight_old, momentum, slot_plan,
    next_input, next_grad,
):
    rows, wcol = first_input.shape[1:3]
    unit = rows * wcol * 9 * C * C
    full = (3, 3, C, C)

    def some(count):
        return ((count, wcol, C), BF16)

    def map_rows(count):
        return pltpu.VMEM((count, wcol, C), BF16)

    def dz_rows(count):
        return pltpu.VMEM((count, wcol, 3 * C), BF16)

    def swapped(array):
        return lax.ppermute(array, "band", SWAP)

    slots = slot_plan.reshape(2)
    edges, mark = call(
        pack, [some(7), ((8, 128), F32)], [SMEM] + hbm(3), vmem(2),
        [pltpu.SemaphoreType.DMA((3,))], 56,
    )(slots, first_input, stashed, first_grad, slots)
    edges = swapped(edges)

    rest, one, two, next_kept, low, high = call(
        pack_rest, [some(2 * rows - 5)] + [some(rows)] * 3 + [some(rows // 2)] * 2,
        [SMEM] + vmem(5), vmem(6), [],
    )(slots, first_input, stashed, first_grad, next_input, next_grad, mark)
    rest = swapped(rest)

    def to_last(array, source, pairs=()):
        last = lax.axis_size("segment") - 1
        pairs = [(2 * (last - source) + at, 2 * last + 1 - at) for at in range(2)] + list(pairs)
        return lax.ppermute(array, ("segment", "band"), pairs)

    low = to_last(low, 4)
    high = to_last(high, 0, SWAP)

    slopes = ((rows - 1, wcol, C), F32)
    y1_far, slope1, slope2, edges2 = call(
        early, [some(rows - 1), slopes, slopes, some(2)],
        vmem(5), vmem(4), [map_rows(rows + 1)] * 3,
    )(one, two, first_input, weight_old, weight_now, two)
    edges2 = swapped(edges2)

    dx_near, y1, rest2, dz3_edge, maps, dz3 = call(
        backward_one,
        [
            some(rows + 1), some(rows + 1), some(rows - 2), ((2, wcol, 3 * C), BF16), some(rows + 4),
            ((rows + 3, wcol, 3 * C), BF16),
        ],
        vmem(9), vmem(6), [map_rows(4)],
    )(one, two, first_input, first_grad, edges, weight_old, weight_now, slope1, y1_far, two)
    returned_near = passed_along(dx_near, "segment", -1)
    x2 = passed_along(y1, "segment", 1)
    rest2 = swapped(rest2)
    (own_kgrad,) = call(own_kernel_grad, [(full, F32)], vmem(2), vmem(1), [])(maps, dz3, dx_near)

    dx_far, maps, dz3, next_grad_other = call(
        backward_one_rest,
        [some(rows - 1), some(rows + 2), ((rows + 1, wcol, 3 * C), BF16), some(rows)],
        vmem(7), vmem(4), [],
    )(one, edges, rest, dz3_edge, weight_old, low, high, own_kgrad)
    returned_far = passed_along(dx_far, "segment", -1)

    m_one, w_one = call(
        update_one, [(full, F32), ((1,) + full, BF16)], vmem(5), vmem(2), [],
    )(maps, dz3, own_kgrad, momentum, weight_now, dx_far)

    dx, own_kgrad, dz3_edge = call(
        backward_two,
        [some(rows), (full, F32), ((1, wcol, 3 * C), BF16)],
        vmem(7), vmem(3),
        [map_rows(rows + 3), map_rows(rows + 1), dz_rows(rows + 2)],
    )(
        two, edges2, returned_near, next_grad, next_grad_other,
        weight_now, slope2, m_one,
    )

    (act,) = call(forward_two, [some(rows)], vmem(4), vmem(1), [map_rows(rows + 2)])(
        next_kept, high, x2, w_one, dz3_edge
    )

    act, dx, m_two, w_two, w_one_out = call(
        finish,
        [((1, rows, wcol, C), BF16)] * 2 + [((1,) + full, F32)] + [((1,) + full, BF16)] * 2,
        vmem(12), hbm(5),
        [
            map_rows(rows + 2), map_rows(rows - 1), dz_rows(rows),
            pltpu.VMEM(full, F32), pltpu.VMEM(full, BF16), pltpu.SemaphoreType.DMA((9,)),
        ],
    )(
        two, edges2, rest2, dz3_edge, returned_far, next_grad_other,
        weight_now, own_kgrad, m_one, w_one, dx, act, act,
    )
    return act, dx, w_two, w_one_out, m_two


def fits_two_bands(mesh):
    return mesh.shape["band"] == 2 and mesh.shape["segment"] >= 8


def solution(mesh):
    placed = (
        P("segment", "band", None, None),
        P("segment", None, "band", None, None),
        P("segment", "band", None, None),
        P("segment", None, None, None, None),
        P("segment", None, None, None, None),
        P("segment", None, None, None, None),
        P(None, "segment"),
        P("band", None, None),
        P("band", None, None),
    )
    return jax.shard_map(
        two_band_body if fits_two_bands(mesh) else body,
        mesh=mesh,
        in_specs=placed,
        out_specs=(
            P("segment", "band", None, None),
            P("segment", "band", None, None),
            P("segment", None, None, None, None),
            P("segment", None, None, None, None),
            P("segment", None, None, None, None),
        ),
        check_vma=False,
    )
```

profile of v0, /device:TPU:27, one launch (start us, length us, event | category | flops | bytes accessed | tf_op | source)
XLA Modules:
  0.0 55.0 jit_solution(3546397823563071586)
XLA Ops:
  0.7 2.8 %pack.1 = (bf16[7,128,256]{2,1,0:T(8,128)(2,1)}, f32[8,128]{1,0:T(8,128)}) custom-call(s32[2]{0:T(128)} %bitcast.1, bf16[1,8,128,256]{3,2,1,0:T(8,128)(2,1)} %refs_2_.7, bf16[1,2,8,128,256]{4,3,2,1,0:T(8,128)(2,1)} %refs_2_.5, bf16[1,8,128,256]{3,2,1,0:T(8,128)(2,1)} %refs_3_.9, s32[2]{0:T(128)} %bitcast.2), custom_call_target="tpu_custom_call" | custom-call | flops 10000000000 | bytes 100000000 | tf_op jit(solution)/shard_map/pack/pallas_call | solution.py:565
  3.5 1.3 %collective-permute-start.1 = (bf16[7,128,256]{2,1,0:T(8,128)(2,1)}, bf16[7,128,256]{2,1,0:T(8,128)(2,1)S(1)}, u32[]{:S(2)}, u32[]{:S(2)}) collective-permute-start(bf16[7,128,256]{2,1,0:T(8,128)(2,1)} %get-tuple-element.41), channel_id=1, source_target_pairs={{0,1},{1,0},{2,3},{3,2},{4,5},{5,4},{6,7},{7,6},{8,9},{9,8},{10,11... | collective-permute-start | bytes 1376264 | tf_op jit(solution)/shard_map/ppermute | solution.py:562
  4.8 0.0 copy-start.9
  4.8 0.7 %copy-done.9 = f32[8,128]{1,0:T(8,128)S(1)} copy-done((f32[8,128]{1,0:T(8,128)S(1)}, f32[8,128]{1,0:T(8,128)}, u32[]{:S(2)}) %copy-start.9) | copy-done | bytes 4120
  5.5 0.7 %pack_rest.1 = (bf16[11,128,256]{2,1,0:T(8,128)(2,1)S(1)}, bf16[8,128,256]{2,1,0:T(8,128)(2,1)S(1)}, bf16[8,128,256]{2,1,0:T(8,128)(2,1)S(1)}, bf16[8,128,256]{2...) custom-call(s32[2]{0:T(128)S(1)} %bitcast.3, ...), custom_call_target="tpu_custom_call" | custom-call | flops 10000000000 | bytes 100000000 | tf_op jit(solution)/shard_map/pack_rest/pallas_call | solution.py:571
  6.2 1.3 %collective-permute-start.5 = (bf16[4,128,256]{2,1,0:T(8,128)(2,1)S(1)}, bf16[4,128,256]{2,1,0:T(8,128)(2,1)S(1)}, u32[]{:S(2)}, u32[]{:S(2)}) collective-permute-start(bf16[4,128,256]{2,1,0:T(8,128)(2,1)S(1)} %get-tuple-element.48), channel_id=1, source_target_pairs={{22,31},{23,30}} | collective-permute-start | bytes 786440 | tf_op jit(solution)/shard_map/ppermute | solution.py:580
  7.5 2.1 %collective-permute-start.6 = (bf16[4,128,256]{2,1,0:T(8,128)(2,1)S(1)}, bf16[4,128,256]{2,1,0:T(8,128)(2,1)S(1)}, u32[]{:S(2)}, u32[]{:S(2)}) collective-permute-start(bf16[4,128,256]{2,1,0:T(8,128)(2,1)S(1)} %get-tuple-element.49), channel_id=1, source_target_pairs={{30,31},{31,30},{0,1},{1,0}} | collective-permute-start | bytes 786440 | tf_op jit(solution)/shard_map/ppermute | solution.py:580
  9.7 1.3 %collective-permute-start.4 = (bf16[11,128,256]{2,1,0:T(8,128)(2,1)S(1)}, bf16[11,128,256]{2,1,0:T(8,128)(2,1)S(1)}, u32[]{:S(2)}, u32[]{:S(2)}) collective-permute-start(bf16[11,128,256]{2,1,0:T(8,128)(2,1)S(1)} %get-tuple-element.46), channel_id=1, source_target_pairs={{0,1},{1,0},{2,3},{3,2},{4,5},{5,4},{6,7},{7,6},{8,9},{9,8},{10,11... | collective-permute-start | bytes 2162696 | tf_op jit(solution)/shard_map/ppermute | solution.py:562
  11.0 6.2 %early.1 = (bf16[7,128,256]{2,1,0:T(8,128)(2,1)S(1)}, f32[7,128,256]{2,1,0:T(8,128)S(1)}, f32[7,128,256]{2,1,0:T(8,128)S(1)}, bf16[2,128,256]{2,1,0:T(8,128)(2,1)S(1)}) custom-call(bf16[8,128,256]{2,1,0:T(8,128)(2,1)S(1)} %get-tuple-element.39.refs_0_, bf16[8,128,256]{2,1,0:T(8,128)(2,1)S(1)} %get-tuple-element.38.refs_1_.refs_5_.refs_9_.refs_0_, ...), custom_call_target="tpu_custom_call" | custom-call | flops 10000000000 | bytes 100000000 | tf_op jit(solution)/shard_map/early/pallas_call | solution.py:586
  17.2 0.3 collective-permute-start
  17.5 0.5 collective-permute-done.1.refs_4_.refs_1_
  17.9 3.1 %backward_one.1 = (bf16[9,128,256]{2,1,0:T(8,128)(2,1)S(1)}, bf16[9,128,256]{2,1,0:T(8,128)(2,1)S(1)}, bf16[6,128,256]{2,1,0:T(8,128)(2,1)S(1)}, bf16[2,128,768]...) custom-call(bf16[8,128,256]{2,1,0:T(8,128)(2,1)S(1)} %get-tuple-element.39.refs_0_, ...), custom_call_target="tpu_custom_call" | custom-call | flops 10000000000 | bytes 100000000 | tf_op jit(solution)/shard_map/backward_one/pallas_call | solution.py:592
  21.0 4.6 %collective-permute-start.3 = (bf16[9,128,256]{2,1,0:T(8,128)(2,1)S(1)}, bf16[9,128,256]{2,1,0:T(8,128)(2,1)S(1)}, u32[]{:S(2)}, u32[]{:S(2)}) collective-permute-start(bf16[9,128,256]{2,1,0:T(8,128)(2,1)S(1)} %get-tuple-element.45.refs_2_), channel_id=1, source_target_pairs={{2,0},{4,2},{6,4},{8,6},{10,8},{12,10},{14,12},{16,14},{18,16},{20... | collective-permute-start | bytes 1769480 | tf_op jit(solution)/shard_map/ppermute | solution.py:30
  25.7 1.9 %own_kernel_grad.1.refs_7_.refs_2_ = f32[3,3,256,256]{3,2,1,0:T(8,128)S(1)} custom-call(bf16[12,128,256]{2,1,0:T(8,128)(2,1)S(1)} %get-tuple-element.50.refs_0_, bf16[11,128,768]{2,1,0:T(8,128)(2,1)S(1)} %get-tuple-element.51.refs_1_, bf16[9,128,256]{2,1,0:T(8,128)(2,1)S(1)} %get-tuple-element.45.refs_2_), custom_call_target="tpu_custom_call" | custom-call | flops 10000000000 | bytes 100000000 | tf_op jit(solution)/shard_map/own_kernel_grad/pallas_call | solution.py:603
  27.5 1.5 %collective-permute-start.2 = (bf16[6,128,256]{2,1,0:T(8,128)(2,1)S(1)}, bf16[6,128,256]{2,1,0:T(8,128)(2,1)S(1)}, u32[]{:S(2)}, u32[]{:S(2)}) collective-permute-start(bf16[6,128,256]{2,1,0:T(8,128)(2,1)S(1)} %get-tuple-element.44), channel_id=1, source_target_pairs={{0,1},{1,0},{2,3},{3,2},{4,5},{5,4},{6,7},{7,6},{8,9},{9,8},{10,11... | collective-permute-start | bytes 1179656 | tf_op jit(solution)/shard_map/ppermute | solution.py:562
  29.0 0.0 collective-permute-done.6.refs_6_.refs_1_
  29.0 1.3 %collective-permute-start.8 = (bf16[9,128,256]{2,1,0:T(8,128)(2,1)S(1)}, bf16[9,128,256]{2,1,0:T(8,128)(2,1)S(1)}, u32[]{:S(2)}, u32[]{:S(2)}) collective-permute-start(bf16[9,128,256]{2,1,0:T(8,128)(2,1)S(1)} %get-tuple-element.63), channel_id=1, source_target_pairs={{0,2},{2,4},{4,6},{6,8},{8,10},{10,12},{12,14},{14,16},{16,18},{18... | collective-permute-start | bytes 1769480 | tf_op jit(solution)/shard_map/ppermute | solution.py:30
  30.3 8.7 %collective-permute-done.4.refs_2_ = bf16[11,128,256]{2,1,0:T(8,128)(2,1)S(1)} collective-permute-done((bf16[11,128,256]{2,1,0:T(8,128)(2,1)S(1)}, bf16[11,128,256]{2,1,0:T(8,128)(2,1)S(1)}, u32[]{:S(2)}, u32[]{:S(2)}) %collective-permute-start.4) | collective-permute-done | bytes 720928 | tf_op jit(solution)/shard_map/ppermute | solution.py:562
  39.0 2.9 %backward_one_rest.1 = (bf16[7,128,256]{2,1,0:T(8,128)(2,1)S(1)}, bf16[10,128,256]{2,1,0:T(8,128)(2,1)S(1)}, bf16[9,128,768]{2,1,0:T(8,128)(2,1)S(1)}, bf16[8,128,256]{2,1,0:T(8,128)(2,1)S(1)}) custom-call(bf16[8,128,256]{2,1,0:T(8,128)(2,1)S(1)} %get-tuple-element.39.refs_0_, bf16[7,128,256]{2,1,0:T(8,128)(2,1)S(1)} %collective-permute-done.1.refs_4_.refs_1_, ...), custom_call_target="tpu_custom_call" | custom-call | flops 10000000000 | bytes 100000000 | tf_op jit(solution)/shard_map/backward_one_rest/pallas_call | solution.py:605
  41.9 1.3 %collective-permute-start.7 = (bf16[7,128,256]{2,1,0:T(8,128)(2,1)S(1)}, bf16[7,128,256]{2,1,0:T(8,128)(2,1)S(1)}, u32[]{:S(2)}, u32[]{:S(2)}) collective-permute-start(bf16[7,128,256]{2,1,0:T(8,128)(2,1)S(1)} %get-tuple-element.56.refs_5_), channel_id=1, source_target_pairs={{2,0},{4,2},{6,4},{8,6},{10,8},{12,10},{14,12},{16,14},{18,16},{20... | collective-permute-start | bytes 1376264 | tf_op jit(solution)/shard_map/ppermute | solution.py:30
  43.3 2.1 %update_one.1 = (f32[3,3,256,256]{3,2,1,0:T(8,128)S(1)}, bf16[1,3,3,256,256]{4,3,2,1,0:T(8,128)(2,1)S(1)}) custom-call(bf16[10,128,256]{2,1,0:T(8,128)(2,1)S(1)} %get-tuple-element.54.refs_0_, bf16[9,128,768]{2,1,0:T(8,128)(2,1)S(1)} %get-tuple-element.55.refs_1_, f32[3,3,256,256]{3,2,1,0:T(8,128)S(1)} %own_kernel_grad.1.refs_7_.refs_2_, ...), custom_call_target="tpu_custom_call" | custom-call | flops 10000000000 | bytes 100000000 | tf_op jit(solution)/shard_map/update_one/pallas_call | solution.py:612
  45.4 3.4 %backward_two.1 = (bf16[8,128,256]{2,1,0:T(8,128)(2,1)S(1)}, f32[3,3,256,256]{3,2,1,0:T(8,128)S(1)}, bf16[1,128,768]{2,1,0:T(8,128)(2,1)S(1)}) custom-call(bf16[8,128,256]{2,1,0:T(8,128)(2,1)S(1)} %get-tuple-element.38.refs_1_.refs_5_.refs_9_.refs_0_, bf16[2,128,256]{2,1,0:T(8,128)(2,1)S(1)} %collective-permute-done.refs_1_, ...), custom_call_target="tpu_custom_call" | custom-call | flops 10000000000 | bytes 100000000 | tf_op jit(solution)/shard_map/backward_two/pallas_call | solution.py:616
  48.9 1.6 %forward_two.1.refs_11_.refs_12_ = bf16[8,128,256]{2,1,0:T(8,128)(2,1)S(1)} custom-call(bf16[8,128,256]{2,1,0:T(8,128)(2,1)S(1)} %get-tuple-element.62.refs_0_, bf16[4,128,256]{2,1,0:T(8,128)(2,1)S(1)} %collective-permute-done.6.refs_6_.refs_1_, bf16[9,128,256]{2,1,0:T(8,128)(2,1)S(1)} %collective-permute-done.8.refs_2_, ...), custom_call_target="tpu_custom_call" | custom-call | flops 10000000000 | bytes 100000000 | tf_op jit(solution)/shard_map/forward_two/pallas_call | solution.py:626
  50.5 4.4 %finish.1 = (bf16[1,8,128,256]{3,2,1,0:T(8,128)(2,1)}, bf16[1,8,128,256]{3,2,1,0:T(8,128)(2,1)}, f32[1,3,3,256,256]{4,3,2,1,0:T(8,128)}, bf16[1,3,3,256,256]{4,3...) custom-call(bf16[8,128,256]{2,1,0:T(8,128)(2,1)S(1)} %get-tuple-element.38.refs_1_.refs_5_.refs_9_.refs_0_, ...), custom_call_target="tpu_custom_call" | custom-call | flops 10000000000 | bytes 100000000 | tf_op jit(solution)/shard_map/finish/pallas_call | solution.py:630
  (24 shorter events, 0.1 us)
Async XLA Ops:
  0.6 4.1 %copy-start.3 = (bf16[1,2,8,128,256]{4,3,2,1,0:T(8,128)(2,1)S(1)}, bf16[1,2,8,128,256]{4,3,2,1,0:T(8,128)(2,1)}, u32[]{:S(2)}) copy-start(bf16[1,2,8,128,256]{4,3,2,1,0:T(8,128)(2,1)} %refs_2_.5) | copy-start | bytes 3145732
  0.6 4.1 %copy-start.4 = (bf16[8,128,256]{2,1,0:T(8,128)(2,1)S(1)}, bf16[8,128,256]{2,1,0:T(8,128)(2,1)}, u32[]{:S(2)}) copy-start(bf16[8,128,256]{2,1,0:T(8,128)(2,1)} %refs_4_.4) | copy-start | bytes 1572868
  0.7 4.1 %copy-start.5 = (bf16[1,8,128,256]{3,2,1,0:T(8,128)(2,1)S(1)}, bf16[1,8,128,256]{3,2,1,0:T(8,128)(2,1)}, u32[]{:S(2)}) copy-start(bf16[1,8,128,256]{3,2,1,0:T(8,128)(2,1)} %refs_2_.7) | copy-start | bytes 1572868
  0.7 4.1 %copy-start.6 = (bf16[1,8,128,256]{3,2,1,0:T(8,128)(2,1)S(1)}, bf16[1,8,128,256]{3,2,1,0:T(8,128)(2,1)}, u32[]{:S(2)}) copy-start(bf16[1,8,128,256]{3,2,1,0:T(8,128)(2,1)} %refs_3_.9) | copy-start | bytes 1572868
  0.7 4.1 %copy-start.7 = (bf16[8,128,256]{2,1,0:T(8,128)(2,1)S(1)}, bf16[8,128,256]{2,1,0:T(8,128)(2,1)}, u32[]{:S(2)}) copy-start(bf16[8,128,256]{2,1,0:T(8,128)(2,1)} %refs_3_.11) | copy-start | bytes 1572868
  0.7 4.1 %copy-start.8 = (s32[2,1]{0,1:T(1,128)S(1)}, s32[2,1]{0,1:T(1,128)}, u32[]{:S(2)}) copy-start(s32[2,1]{0,1:T(1,128)} %param.15) | copy-start | bytes 28
  3.5 14.5 %collective-permute-start.1 = (bf16[7,128,256]{2,1,0:T(8,128)(2,1)}, bf16[7,128,256]{2,1,0:T(8,128)(2,1)S(1)}, u32[]{:S(2)}, u32[]{:S(2)}) collective-permute-start(bf16[7,128,256]{2,1,0:T(8,128)(2,1)} %get-tuple-element.41), channel_id=1, source_target_pairs={{0,1},{1,0},{2,3},{3,2},{4,5},{5,4},{6,7},{7,6},{8,9},{9,8},{10,11... | collective-permute-start | bytes 1376264 | tf_op jit(solution)/shard_map/ppermute | solution.py:562
  4.8 0.7 %copy-start.9 = (f32[8,128]{1,0:T(8,128)S(1)}, f32[8,128]{1,0:T(8,128)}, u32[]{:S(2)}) copy-start(f32[8,128]{1,0:T(8,128)} %get-tuple-element.37.refs_6_) | copy-start | bytes 12292
  5.5 5.5 %copy-start.1 = (bf16[1,3,3,256,256]{4,3,2,1,0:T(8,128)(2,1)S(1)}, bf16[1,3,3,256,256]{4,3,2,1,0:T(8,128)(2,1)}, u32[]{:S(2)}) copy-start(bf16[1,3,3,256,256]{4,3,2,1,0:T(8,128)(2,1)} %refs_4_.6) | copy-start | bytes 3538948
  5.5 5.5 %copy-start.2 = (bf16[1,3,3,256,256]{4,3,2,1,0:T(8,128)(2,1)S(1)}, bf16[1,3,3,256,256]{4,3,2,1,0:T(8,128)(2,1)}, u32[]{:S(2)}) copy-start(bf16[1,3,3,256,256]{4,3,2,1,0:T(8,128)(2,1)} %refs_6_.3) | copy-start | bytes 3538948
  6.2 21.3 %collective-permute-start.5 = (bf16[4,128,256]{2,1,0:T(8,128)(2,1)S(1)}, bf16[4,128,256]{2,1,0:T(8,128)(2,1)S(1)}, u32[]{:S(2)}, u32[]{:S(2)}) collective-permute-start(bf16[4,128,256]{2,1,0:T(8,128)(2,1)S(1)} %get-tuple-element.48), channel_id=1, source_target_pairs={{22,31},{23,30}} | collective-permute-start | bytes 786440 | tf_op jit(solution)/shard_map/ppermute | solution.py:580
  7.5 21.5 %collective-permute-start.6 = (bf16[4,128,256]{2,1,0:T(8,128)(2,1)S(1)}, bf16[4,128,256]{2,1,0:T(8,128)(2,1)S(1)}, u32[]{:S(2)}, u32[]{:S(2)}) collective-permute-start(bf16[4,128,256]{2,1,0:T(8,128)(2,1)S(1)} %get-tuple-element.49), channel_id=1, source_target_pairs={{30,31},{31,30},{0,1},{1,0}} | collective-permute-start | bytes 786440 | tf_op jit(solution)/shard_map/ppermute | solution.py:580
  9.7 29.3 %collective-permute-start.4 = (bf16[11,128,256]{2,1,0:T(8,128)(2,1)S(1)}, bf16[11,128,256]{2,1,0:T(8,128)(2,1)S(1)}, u32[]{:S(2)}, u32[]{:S(2)}) collective-permute-start(bf16[11,128,256]{2,1,0:T(8,128)(2,1)S(1)} %get-tuple-element.46), channel_id=1, source_target_pairs={{0,1},{1,0},{2,3},{3,2},{4,5},{5,4},{6,7},{7,6},{8,9},{9,8},{10,11... | collective-permute-start | bytes 2162696 | tf_op jit(solution)/shard_map/ppermute | solution.py:562
  17.2 28.2 %collective-permute-start = (bf16[2,128,256]{2,1,0:T(8,128)(2,1)S(1)}, bf16[2,128,256]{2,1,0:T(8,128)(2,1)S(1)}, u32[]{:S(2)}, u32[]{:S(2)}) collective-permute-start(bf16[2,128,256]{2,1,0:T(8,128)(2,1)S(1)} %get-tuple-element.40), channel_id=1, source_target_pairs={{0,1},{1,0},{2,3},{3,2},{4,5},{5,4},{6,7},{7,6},{8,9},{9,8},{10,11... | collective-permute-start | bytes 393224 | tf_op jit(solution)/shard_map/ppermute | solution.py:562
  21.0 24.4 %collective-permute-start.3 = (bf16[9,128,256]{2,1,0:T(8,128)(2,1)S(1)}, bf16[9,128,256]{2,1,0:T(8,128)(2,1)S(1)}, u32[]{:S(2)}, u32[]{:S(2)}) collective-permute-start(bf16[9,128,256]{2,1,0:T(8,128)(2,1)S(1)} %get-tuple-element.45.refs_2_), channel_id=1, source_target_pairs={{2,0},{4,2},{6,4},{8,6},{10,8},{12,10},{14,12},{16,14},{18,16},{20... | collective-permute-start | bytes 1769480 | tf_op jit(solution)/shard_map/ppermute | solution.py:30
  27.5 22.9 %collective-permute-start.2 = (bf16[6,128,256]{2,1,0:T(8,128)(2,1)S(1)}, bf16[6,128,256]{2,1,0:T(8,128)(2,1)S(1)}, u32[]{:S(2)}, u32[]{:S(2)}) collective-permute-start(bf16[6,128,256]{2,1,0:T(8,128)(2,1)S(1)} %get-tuple-element.44), channel_id=1, source_target_pairs={{0,1},{1,0},{2,3},{3,2},{4,5},{5,4},{6,7},{7,6},{8,9},{9,8},{10,11... | collective-permute-start | bytes 1179656 | tf_op jit(solution)/shard_map/ppermute | solution.py:562
  29.0 19.8 %collective-permute-start.8 = (bf16[9,128,256]{2,1,0:T(8,128)(2,1)S(1)}, bf16[9,128,256]{2,1,0:T(8,128)(2,1)S(1)}, u32[]{:S(2)}, u32[]{:S(2)}) collective-permute-start(bf16[9,128,256]{2,1,0:T(8,128)(2,1)S(1)} %get-tuple-element.63), channel_id=1, source_target_pairs={{0,2},{2,4},{4,6},{6,8},{8,10},{10,12},{12,14},{14,16},{16,18},{18... | collective-permute-start | bytes 1769480 | tf_op jit(solution)/shard_map/ppermute | solution.py:30
  39.0 4.3 %copy-start = (f32[1,3,3,256,256]{4,3,2,1,0:T(8,128)S(1)}, f32[1,3,3,256,256]{4,3,2,1,0:T(8,128)}, u32[]{:S(2)}) copy-start(f32[1,3,3,256,256]{4,3,2,1,0:T(8,128)} %refs_3_.10) | copy-start | bytes 7077892
  41.9 8.5 %collective-permute-start.7 = (bf16[7,128,256]{2,1,0:T(8,128)(2,1)S(1)}, bf16[7,128,256]{2,1,0:T(8,128)(2,1)S(1)}, u32[]{:S(2)}, u32[]{:S(2)}) collective-permute-start(bf16[7,128,256]{2,1,0:T(8,128)(2,1)S(1)} %get-tuple-element.56.refs_5_), channel_id=1, source_target_pairs={{2,0},{4,2},{6,4},{8,6},{10,8},{12,10},{14,12},{16,14},{18,16},{20... | collective-permute-start | bytes 1376264 | tf_op jit(solution)/shard_map/ppermute | solution.py:30
where the time goes:
time: 56.1 us; the launch traced here: 55 us
  Pallas kernels  29.1 us (52%)
  starting transfers between devices  15.1 us (27%)
  waiting for transfers between devices  9.14 us (16%)
  between operations  1.04 us (2%)
  local copies, waits for them, and re-layouts  0.72 us (1%)
    ppermute x4, waiting for transfers between devices, swapped(): return lax.ppermute(array, 'band', SWAP)  9.13 us
    ppermute x3, starting transfers between devices, passed_along(): return lax.ppermute(array, axis, pairs)  7.24 us
    pallas_call x1, Pallas kernels, two_band_body(): call(early, [some(rows - 1), slopes, slopes, some(2)], vmem(5), vmem(4),...  6.19 us
    pallas_call x1, Pallas kernels, two_band_body(): call(finish, [((1, rows, wcol, C), BF16)] * 2 + [((1,) + full, F32)] + [(...  4.4 us
    ppermute x4, starting transfers between devices, swapped(): return lax.ppermute(array, 'band', SWAP)  4.4 us
    pallas_call x1, Pallas kernels, two_band_body(): call(backward_two, [some(rows), (full, F32), ((1, wcol, 3 * C), BF16)], v...  3.44 us
    ppermute x2, starting transfers between devices, to_last(): return lax.ppermute(array, ('segment', 'band'), pairs)  3.43 us
    pallas_call x1, Pallas kernels, two_band_body(): call(backward_one, [some(rows + 1), some(rows + 1), some(rows - 2), ((2,...  3.07 us
  transfers between devices with their start and end apart: 9, of which 2 were waited for; matrix products, arithmetic and copies ran while one was open for 0% of the time, Pallas kernels for 40%

commit v1 on v0

--- a/solution.py
+++ b/solution.py
@@ -335,15 +335,15 @@
     rest[rows - 3 :] = grad[0, inner(rows, rows - 2, me)]
     next_kept[...] = next_in[...]
     first = lax.axis_index("segment") == 0
-    low[...] = next_g[0 : rows // 2]
+    low[...] = next_g[0 : rows - 2]
 
     @pl.when(first)
     def _():
-        high[...] = next_in[edge(rows, rows // 2, me)]
+        high[...] = next_in[edge(rows, 2, me)]
 
     @pl.when(jnp.logical_not(first))
     def _():
-        high[...] = next_g[rows // 2 :]
+        high[...] = next_g[rows - 2 :]
 
 
 def early(
@@ -380,7 +380,7 @@
     @pl.when(first)
     def _():
         put(maps, 1, next_in[...])
-        put(maps, (rows + 1) * (1 - me), beside[pl.ds((rows // 2 - 1) * me, 1)])
+        put(maps, (rows + 1) * (1 - me), beside[pl.ds(me, 1)])
 
     @pl.when(jnp.logical_not(first))
     def _():
@@ -437,7 +437,7 @@
     rows = one.shape[0]
     zero_row(maps, (rows + 1) * (1 - me))
     put(next_g_other, 0, low[...])
-    put(next_g_other, rows // 2, high[...])
+    put(next_g_other, rows - 2, high[...])
     put(maps, (rows + 1) * me, one[edge(rows, 1, me)])
     put(maps, 1 + (rows - 3) * me, edges[0:3])
     put(maps, 4 - 3 * me, rest[0 : rows - 3])
@@ -569,7 +569,7 @@
     edges = swapped(edges)
 
     rest, one, two, next_kept, low, high = call(
-        pack_rest, [some(2 * rows - 5)] + [some(rows)] * 3 + [some(rows // 2)] * 2,
+        pack_rest, [some(2 * rows - 5)] + [some(rows)] * 3 + [some(rows - 2), some(2)],
         [SMEM] + vmem(5), vmem(6), [],
     )(slots, first_input, stashed, first_grad, next_input, next_grad, mark)
     rest = swapped(rest)
@@ -579,7 +579,7 @@
         pairs = [(2 * (last - source) + at, 2 * last + 1 - at) for at in range(2)] + list(pairs)
         return lax.ppermute(array, ("segment", "band"), pairs)
 
-    low = to_last(low, 4)
+    low = to_last(low, 2)
     high = to_last(high, 0, SWAP)
 
     slopes = ((rows - 1, wcol, C), F32)

time: 56.1 us -> 54.5 us (0.971); the launches traced: 55 us -> 54.1 us
  waiting for transfers between devices: 9.14 us -> 7.74 us
    ppermute x4, waiting for transfers between devices: 9.13 us -> 7.73 us  [swapped(): return lax.ppermute(array, 'band', SWAP)]
where the time goes in v1:
time: 54.5 us; the launch traced here: 54.1 us
  Pallas kernels  29.1 us (53%)
  starting transfers between devices  15.6 us (29%)
  waiting for transfers between devices  7.74 us (14%)
  between operations  1.04 us (2%)
  local copies, waits for them, and re-layouts  0.72 us (1%)
    ppermute x3, starting transfers between devices, passed_along(): return lax.ppermute(array, axis, pairs)  7.74 us
    ppermute x4, waiting for transfers between devices, swapped(): return lax.ppermute(array, 'band', SWAP)  7.73 us
    pallas_call x1, Pallas kernels, two_band_body(): call(early, [some(rows - 1), slopes, slopes, some(2)], vmem(5), vmem(4),...  6.19 us
    pallas_call x1, Pallas kernels, two_band_body(): call(finish, [((1, rows, wcol, C), BF16)] * 2 + [((1,) + full, F32)] + [(...  4.4 us
    ppermute x4, starting transfers between devices, swapped(): return lax.ppermute(array, 'band', SWAP)  4.4 us
    pallas_call x1, Pallas kernels, two_band_body(): call(backward_two, [some(rows), (full, F32), ((1, wcol, 3 * C), BF16)], v...  3.44 us
    ppermute x2, starting transfers between devices, to_last(): return lax.ppermute(array, ('segment', 'band'), pairs)  3.43 us
    pallas_call x1, Pallas kernels, two_band_body(): call(backward_one, [some(rows + 1), some(rows + 1), some(rows - 2), ((2,...  3.07 us
  transfers between devices with their start and end apart: 9, of which 2 were waited for; matrix products, arithmetic and copies ran while one was open for 0% of the time, Pallas kernels for 40%

profile of v1, /device:TPU:27, one launch (start us, length us, event | category | flops | bytes accessed | tf_op | source)
XLA Modules:
  0.0 54.1 jit_solution(8145918751713510885)
XLA Ops:
  0.7 2.8 %pack.1 = (bf16[7,128,256]{2,1,0:T(8,128)(2,1)}, f32[8,128]{1,0:T(8,128)}) custom-call(s32[2]{0:T(128)} %bitcast.1, bf16[1,8,128,256]{3,2,1,0:T(8,128)(2,1)} %refs_2_.7, bf16[1,2,8,128,256]{4,3,2,1,0:T(8,128)(2,1)} %refs_2_.5, bf16[1,8,128,256]{3,2,1,0:T(8,128)(2,1)} %refs_3_.9, s32[2]{0:T(128)} %bitcast.2), custom_call_target="tpu_custom_call" | custom-call | flops 10000000000 | bytes 100000000 | tf_op jit(solution)/shard_map/pack/pallas_call | solution.py:565
  3.5 1.3 %collective-permute-start.1 = (bf16[7,128,256]{2,1,0:T(8,128)(2,1)}, bf16[7,128,256]{2,1,0:T(8,128)(2,1)S(1)}, u32[]{:S(2)}, u32[]{:S(2)}) collective-permute-start(bf16[7,128,256]{2,1,0:T(8,128)(2,1)} %get-tuple-element.41), channel_id=1, source_target_pairs={{0,1},{1,0},{2,3},{3,2},{4,5},{5,4},{6,7},{7,6},{8,9},{9,8},{10,11... | collective-permute-start | bytes 1376264 | tf_op jit(solution)/shard_map/ppermute | solution.py:562
  4.8 0.0 copy-start.9
  4.8 0.7 %copy-done.9 = f32[8,128]{1,0:T(8,128)S(1)} copy-done((f32[8,128]{1,0:T(8,128)S(1)}, f32[8,128]{1,0:T(8,128)}, u32[]{:S(2)}) %copy-start.9) | copy-done | bytes 4120
  5.5 0.7 %pack_rest.1 = (bf16[11,128,256]{2,1,0:T(8,128)(2,1)S(1)}, bf16[8,128,256]{2,1,0:T(8,128)(2,1)S(1)}, bf16[8,128,256]{2,1,0:T(8,128)(2,1)S(1)}, bf16[8,128,256]{2...) custom-call(s32[2]{0:T(128)S(1)} %bitcast.3, ...), custom_call_target="tpu_custom_call" | custom-call | flops 10000000000 | bytes 100000000 | tf_op jit(solution)/shard_map/pack_rest/pallas_call | solution.py:571
  6.2 2.1 %collective-permute-start.6 = (bf16[2,128,256]{2,1,0:T(8,128)(2,1)S(1)}, bf16[2,128,256]{2,1,0:T(8,128)(2,1)S(1)}, u32[]{:S(2)}, u32[]{:S(2)}) collective-permute-start(bf16[2,128,256]{2,1,0:T(8,128)(2,1)S(1)} %get-tuple-element.49), channel_id=1, source_target_pairs={{30,31},{31,30},{0,1},{1,0}} | collective-permute-start | bytes 393224 | tf_op jit(solution)/shard_map/ppermute | solution.py:580
  8.4 1.3 %collective-permute-start.5 = (bf16[6,128,256]{2,1,0:T(8,128)(2,1)S(1)}, bf16[6,128,256]{2,1,0:T(8,128)(2,1)S(1)}, u32[]{:S(2)}, u32[]{:S(2)}) collective-permute-start(bf16[6,128,256]{2,1,0:T(8,128)(2,1)S(1)} %get-tuple-element.48), channel_id=1, source_target_pairs={{26,31},{27,30}} | collective-permute-start | bytes 1179656 | tf_op jit(solution)/shard_map/ppermute | solution.py:580
  9.7 1.3 %collective-permute-start.4 = (bf16[11,128,256]{2,1,0:T(8,128)(2,1)S(1)}, bf16[11,128,256]{2,1,0:T(8,128)(2,1)S(1)}, u32[]{:S(2)}, u32[]{:S(2)}) collective-permute-start(bf16[11,128,256]{2,1,0:T(8,128)(2,1)S(1)} %get-tuple-element.46), channel_id=1, source_target_pairs={{0,1},{1,0},{2,3},{3,2},{4,5},{5,4},{6,7},{7,6},{8,9},{9,8},{10,11... | collective-permute-start | bytes 2162696 | tf_op jit(solution)/shard_map/ppermute | solution.py:562
  11.0 6.2 %early.1 = (bf16[7,128,256]{2,1,0:T(8,128)(2,1)S(1)}, f32[7,128,256]{2,1,0:T(8,128)S(1)}, f32[7,128,256]{2,1,0:T(8,128)S(1)}, bf16[2,128,256]{2,1,0:T(8,128)(2,1)S(1)}) custom-call(bf16[8,128,256]{2,1,0:T(8,128)(2,1)S(1)} %get-tuple-element.39.refs_0_, bf16[8,128,256]{2,1,0:T(8,128)(2,1)S(1)} %get-tuple-element.38.refs_1_.refs_5_.refs_9_.refs_0_, ...), custom_call_target="tpu_custom_call" | custom-call | flops 10000000000 | bytes 100000000 | tf_op jit(solution)/shard_map/early/pallas_call | solution.py:586
  17.2 0.3 collective-permute-start
  17.5 1.9 %collective-permute-done.1.refs_4_.refs_1_ = bf16[7,128,256]{2,1,0:T(8,128)(2,1)S(1)} collective-permute-done((bf16[7,128,256]{2,1,0:T(8,128)(2,1)}, bf16[7,128,256]{2,1,0:T(8,128)(2,1)S(1)}, u32[]{:S(2)}, u32[]{:S(2)}) %collective-permute-start.1) | collective-permute-done | bytes 458784 | tf_op jit(solution)/shard_map/ppermute | solution.py:562
  19.3 3.1 %backward_one.1 = (bf16[9,128,256]{2,1,0:T(8,128)(2,1)S(1)}, bf16[9,128,256]{2,1,0:T(8,128)(2,1)S(1)}, bf16[6,128,256]{2,1,0:T(8,128)(2,1)S(1)}, bf16[2,128,768]...) custom-call(bf16[8,128,256]{2,1,0:T(8,128)(2,1)S(1)} %get-tuple-element.39.refs_0_, ...), custom_call_target="tpu_custom_call" | custom-call | flops 10000000000 | bytes 100000000 | tf_op jit(solution)/shard_map/backward_one/pallas_call | solution.py:592
  22.4 4.6 %collective-permute-start.3 = (bf16[9,128,256]{2,1,0:T(8,128)(2,1)S(1)}, bf16[9,128,256]{2,1,0:T(8,128)(2,1)S(1)}, u32[]{:S(2)}, u32[]{:S(2)}) collective-permute-start(bf16[9,128,256]{2,1,0:T(8,128)(2,1)S(1)} %get-tuple-element.45.refs_2_), channel_id=1, source_target_pairs={{2,0},{4,2},{6,4},{8,6},{10,8},{12,10},{14,12},{16,14},{18,16},{20... | collective-permute-start | bytes 1769480 | tf_op jit(solution)/shard_map/ppermute | solution.py:30
  27.1 1.9 %own_kernel_grad.1.refs_7_.refs_2_ = f32[3,3,256,256]{3,2,1,0:T(8,128)S(1)} custom-call(bf16[12,128,256]{2,1,0:T(8,128)(2,1)S(1)} %get-tuple-element.50.refs_0_, bf16[11,128,768]{2,1,0:T(8,128)(2,1)S(1)} %get-tuple-element.51.refs_1_, bf16[9,128,256]{2,1,0:T(8,128)(2,1)S(1)} %get-tuple-element.45.refs_2_), custom_call_target="tpu_custom_call" | custom-call | flops 10000000000 | bytes 100000000 | tf_op jit(solution)/shard_map/own_kernel_grad/pallas_call | solution.py:603
  28.9 0.0 collective-permute-done.6.refs_6_.refs_1_
  28.9 1.5 %collective-permute-start.2 = (bf16[6,128,256]{2,1,0:T(8,128)(2,1)S(1)}, bf16[6,128,256]{2,1,0:T(8,128)(2,1)S(1)}, u32[]{:S(2)}, u32[]{:S(2)}) collective-permute-start(bf16[6,128,256]{2,1,0:T(8,128)(2,1)S(1)} %get-tuple-element.44), channel_id=1, source_target_pairs={{0,1},{1,0},{2,3},{3,2},{4,5},{5,4},{6,7},{7,6},{8,9},{9,8},{10,11... | collective-permute-start | bytes 1179656 | tf_op jit(solution)/shard_map/ppermute | solution.py:562
  30.4 1.3 %collective-permute-start.8 = (bf16[9,128,256]{2,1,0:T(8,128)(2,1)S(1)}, bf16[9,128,256]{2,1,0:T(8,128)(2,1)S(1)}, u32[]{:S(2)}, u32[]{:S(2)}) collective-permute-start(bf16[9,128,256]{2,1,0:T(8,128)(2,1)S(1)} %get-tuple-element.63), channel_id=1, source_target_pairs={{0,2},{2,4},{4,6},{6,8},{8,10},{10,12},{12,14},{14,16},{16,18},{18... | collective-permute-start | bytes 1769480 | tf_op jit(solution)/shard_map/ppermute | solution.py:30
  31.7 5.9 %collective-permute-done.4.refs_2_ = bf16[11,128,256]{2,1,0:T(8,128)(2,1)S(1)} collective-permute-done((bf16[11,128,256]{2,1,0:T(8,128)(2,1)S(1)}, bf16[11,128,256]{2,1,0:T(8,128)(2,1)S(1)}, u32[]{:S(2)}, u32[]{:S(2)}) %collective-permute-start.4) | collective-permute-done | bytes 720928 | tf_op jit(solution)/shard_map/ppermute | solution.py:562
  37.6 2.9 %backward_one_rest.1 = (bf16[7,128,256]{2,1,0:T(8,128)(2,1)S(1)}, bf16[10,128,256]{2,1,0:T(8,128)(2,1)S(1)}, bf16[9,128,768]{2,1,0:T(8,128)(2,1)S(1)}, bf16[8,128,256]{2,1,0:T(8,128)(2,1)S(1)}) custom-call(bf16[8,128,256]{2,1,0:T(8,128)(2,1)S(1)} %get-tuple-element.39.refs_0_, bf16[7,128,256]{2,1,0:T(8,128)(2,1)S(1)} %collective-permute-done.1.refs_4_.refs_1_, ...), custom_call_target="tpu_custom_call" | custom-call | flops 10000000000 | bytes 100000000 | tf_op jit(solution)/shard_map/backward_one_rest/pallas_call | solution.py:605
  40.5 1.8 %collective-permute-start.7 = (bf16[7,128,256]{2,1,0:T(8,128)(2,1)S(1)}, bf16[7,128,256]{2,1,0:T(8,128)(2,1)S(1)}, u32[]{:S(2)}, u32[]{:S(2)}) collective-permute-start(bf16[7,128,256]{2,1,0:T(8,128)(2,1)S(1)} %get-tuple-element.56.refs_5_), channel_id=1, source_target_pairs={{2,0},{4,2},{6,4},{8,6},{10,8},{12,10},{14,12},{16,14},{18,16},{20... | collective-permute-start | bytes 1376264 | tf_op jit(solution)/shard_map/ppermute | solution.py:30
  42.4 2.1 %update_one.1 = (f32[3,3,256,256]{3,2,1,0:T(8,128)S(1)}, bf16[1,3,3,256,256]{4,3,2,1,0:T(8,128)(2,1)S(1)}) custom-call(bf16[10,128,256]{2,1,0:T(8,128)(2,1)S(1)} %get-tuple-element.54.refs_0_, bf16[9,128,768]{2,1,0:T(8,128)(2,1)S(1)} %get-tuple-element.55.refs_1_, f32[3,3,256,256]{3,2,1,0:T(8,128)S(1)} %own_kernel_grad.1.refs_7_.refs_2_, ...), custom_call_target="tpu_custom_call" | custom-call | flops 10000000000 | bytes 100000000 | tf_op jit(solution)/shard_map/update_one/pallas_call | solution.py:612
  44.5 3.4 %backward_two.1 = (bf16[8,128,256]{2,1,0:T(8,128)(2,1)S(1)}, f32[3,3,256,256]{3,2,1,0:T(8,128)S(1)}, bf16[1,128,768]{2,1,0:T(8,128)(2,1)S(1)}) custom-call(bf16[8,128,256]{2,1,0:T(8,128)(2,1)S(1)} %get-tuple-element.38.refs_1_.refs_5_.refs_9_.refs_0_, bf16[2,128,256]{2,1,0:T(8,128)(2,1)S(1)} %collective-permute-done.refs_1_, ...), custom_call_target="tpu_custom_call" | custom-call | flops 10000000000 | bytes 100000000 | tf_op jit(solution)/shard_map/backward_two/pallas_call | solution.py:616
  48.0 1.6 %forward_two.1.refs_11_.refs_12_ = bf16[8,128,256]{2,1,0:T(8,128)(2,1)S(1)} custom-call(bf16[8,128,256]{2,1,0:T(8,128)(2,1)S(1)} %get-tuple-element.62.refs_0_, bf16[2,128,256]{2,1,0:T(8,128)(2,1)S(1)} %collective-permute-done.6.refs_6_.refs_1_, bf16[9,128,256]{2,1,0:T(8,128)(2,1)S(1)} %collective-permute-done.8.refs_2_, ...), custom_call_target="tpu_custom_call" | custom-call | flops 10000000000 | bytes 100000000 | tf_op jit(solution)/shard_map/forward_two/pallas_call | solution.py:626
  49.6 4.4 %finish.1 = (bf16[1,8,128,256]{3,2,1,0:T(8,128)(2,1)}, bf16[1,8,128,256]{3,2,1,0:T(8,128)(2,1)}, f32[1,3,3,256,256]{4,3,2,1,0:T(8,128)}, bf16[1,3,3,256,256]{4,3...) custom-call(bf16[8,128,256]{2,1,0:T(8,128)(2,1)S(1)} %get-tuple-element.38.refs_1_.refs_5_.refs_9_.refs_0_, ...), custom_call_target="tpu_custom_call" | custom-call | flops 10000000000 | bytes 100000000 | tf_op jit(solution)/shard_map/finish/pallas_call | solution.py:630
  (24 shorter events, 0.1 us)
Async XLA Ops:
  0.6 4.1 %copy-start.3 = (bf16[1,2,8,128,256]{4,3,2,1,0:T(8,128)(2,1)S(1)}, bf16[1,2,8,128,256]{4,3,2,1,0:T(8,128)(2,1)}, u32[]{:S(2)}) copy-start(bf16[1,2,8,128,256]{4,3,2,1,0:T(8,128)(2,1)} %refs_2_.5) | copy-start | bytes 3145732
  0.6 4.1 %copy-start.4 = (bf16[8,128,256]{2,1,0:T(8,128)(2,1)S(1)}, bf16[8,128,256]{2,1,0:T(8,128)(2,1)}, u32[]{:S(2)}) copy-start(bf16[8,128,256]{2,1,0:T(8,128)(2,1)} %refs_4_.4) | copy-start | bytes 1572868
  0.7 4.1 %copy-start.5 = (bf16[1,8,128,256]{3,2,1,0:T(8,128)(2,1)S(1)}, bf16[1,8,128,256]{3,2,1,0:T(8,128)(2,1)}, u32[]{:S(2)}) copy-start(bf16[1,8,128,256]{3,2,1,0:T(8,128)(2,1)} %refs_2_.7) | copy-start | bytes 1572868
  0.7 4.1 %copy-start.6 = (bf16[1,8,128,256]{3,2,1,0:T(8,128)(2,1)S(1)}, bf16[1,8,128,256]{3,2,1,0:T(8,128)(2,1)}, u32[]{:S(2)}) copy-start(bf16[1,8,128,256]{3,2,1,0:T(8,128)(2,1)} %refs_3_.9) | copy-start | bytes 1572868
  0.7 4.1 %copy-start.7 = (bf16[8,128,256]{2,1,0:T(8,128)(2,1)S(1)}, bf16[8,128,256]{2,1,0:T(8,128)(2,1)}, u32[]{:S(2)}) copy-start(bf16[8,128,256]{2,1,0:T(8,128)(2,1)} %refs_3_.11) | copy-start | bytes 1572868
  0.7 4.1 %copy-start.8 = (s32[2,1]{0,1:T(1,128)S(1)}, s32[2,1]{0,1:T(1,128)}, u32[]{:S(2)}) copy-start(s32[2,1]{0,1:T(1,128)} %param.15) | copy-start | bytes 28
  3.5 15.9 %collective-permute-start.1 = (bf16[7,128,256]{2,1,0:T(8,128)(2,1)}, bf16[7,128,256]{2,1,0:T(8,128)(2,1)S(1)}, u32[]{:S(2)}, u32[]{:S(2)}) collective-permute-start(bf16[7,128,256]{2,1,0:T(8,128)(2,1)} %get-tuple-element.41), channel_id=1, source_target_pairs={{0,1},{1,0},{2,3},{3,2},{4,5},{5,4},{6,7},{7,6},{8,9},{9,8},{10,11... | collective-permute-start | bytes 1376264 | tf_op jit(solution)/shard_map/ppermute | solution.py:562
  4.8 0.7 %copy-start.9 = (f32[8,128]{1,0:T(8,128)S(1)}, f32[8,128]{1,0:T(8,128)}, u32[]{:S(2)}) copy-start(f32[8,128]{1,0:T(8,128)} %get-tuple-element.37.refs_6_) | copy-start | bytes 12292
  5.5 5.5 %copy-start.1 = (bf16[1,3,3,256,256]{4,3,2,1,0:T(8,128)(2,1)S(1)}, bf16[1,3,3,256,256]{4,3,2,1,0:T(8,128)(2,1)}, u32[]{:S(2)}) copy-start(bf16[1,3,3,256,256]{4,3,2,1,0:T(8,128)(2,1)} %refs_4_.6) | copy-start | bytes 3538948
  5.5 5.5 %copy-start.2 = (bf16[1,3,3,256,256]{4,3,2,1,0:T(8,128)(2,1)S(1)}, bf16[1,3,3,256,256]{4,3,2,1,0:T(8,128)(2,1)}, u32[]{:S(2)}) copy-start(bf16[1,3,3,256,256]{4,3,2,1,0:T(8,128)(2,1)} %refs_6_.3) | copy-start | bytes 3538948
  6.2 22.7 %collective-permute-start.6 = (bf16[2,128,256]{2,1,0:T(8,128)(2,1)S(1)}, bf16[2,128,256]{2,1,0:T(8,128)(2,1)S(1)}, u32[]{:S(2)}, u32[]{:S(2)}) collective-permute-start(bf16[2,128,256]{2,1,0:T(8,128)(2,1)S(1)} %get-tuple-element.49), channel_id=1, source_target_pairs={{30,31},{31,30},{0,1},{1,0}} | collective-permute-start | bytes 393224 | tf_op jit(solution)/shard_map/ppermute | solution.py:580
  8.4 22.1 %collective-permute-start.5 = (bf16[6,128,256]{2,1,0:T(8,128)(2,1)S(1)}, bf16[6,128,256]{2,1,0:T(8,128)(2,1)S(1)}, u32[]{:S(2)}, u32[]{:S(2)}) collective-permute-start(bf16[6,128,256]{2,1,0:T(8,128)(2,1)S(1)} %get-tuple-element.48), channel_id=1, source_target_pairs={{26,31},{27,30}} | collective-permute-start | bytes 1179656 | tf_op jit(solution)/shard_map/ppermute | solution.py:580
  9.7 27.9 %collective-permute-start.4 = (bf16[11,128,256]{2,1,0:T(8,128)(2,1)S(1)}, bf16[11,128,256]{2,1,0:T(8,128)(2,1)S(1)}, u32[]{:S(2)}, u32[]{:S(2)}) collective-permute-start(bf16[11,128,256]{2,1,0:T(8,128)(2,1)S(1)} %get-tuple-element.46), channel_id=1, source_target_pairs={{0,1},{1,0},{2,3},{3,2},{4,5},{5,4},{6,7},{7,6},{8,9},{9,8},{10,11... | collective-permute-start | bytes 2162696 | tf_op jit(solution)/shard_map/ppermute | solution.py:562
  17.2 27.3 %collective-permute-start = (bf16[2,128,256]{2,1,0:T(8,128)(2,1)S(1)}, bf16[2,128,256]{2,1,0:T(8,128)(2,1)S(1)}, u32[]{:S(2)}, u32[]{:S(2)}) collective-permute-start(bf16[2,128,256]{2,1,0:T(8,128)(2,1)S(1)} %get-tuple-element.40), channel_id=1, source_target_pairs={{0,1},{1,0},{2,3},{3,2},{4,5},{5,4},{6,7},{7,6},{8,9},{9,8},{10,11... | collective-permute-start | bytes 393224 | tf_op jit(solution)/shard_map/ppermute | solution.py:562
  22.4 22.1 %collective-permute-start.3 = (bf16[9,128,256]{2,1,0:T(8,128)(2,1)S(1)}, bf16[9,128,256]{2,1,0:T(8,128)(2,1)S(1)}, u32[]{:S(2)}, u32[]{:S(2)}) collective-permute-start(bf16[9,128,256]{2,1,0:T(8,128)(2,1)S(1)} %get-tuple-element.45.refs_2_), channel_id=1, source_target_pairs={{2,0},{4,2},{6,4},{8,6},{10,8},{12,10},{14,12},{16,14},{18,16},{20... | collective-permute-start | bytes 1769480 | tf_op jit(solution)/shard_map/ppermute | solution.py:30
  28.9 20.6 %collective-permute-start.2 = (bf16[6,128,256]{2,1,0:T(8,128)(2,1)S(1)}, bf16[6,128,256]{2,1,0:T(8,128)(2,1)S(1)}, u32[]{:S(2)}, u32[]{:S(2)}) collective-permute-start(bf16[6,128,256]{2,1,0:T(8,128)(2,1)S(1)} %get-tuple-element.44), channel_id=1, source_target_pairs={{0,1},{1,0},{2,3},{3,2},{4,5},{5,4},{6,7},{7,6},{8,9},{9,8},{10,11... | collective-permute-start | bytes 1179656 | tf_op jit(solution)/shard_map/ppermute | solution.py:562
  30.4 17.5 %collective-permute-start.8 = (bf16[9,128,256]{2,1,0:T(8,128)(2,1)S(1)}, bf16[9,128,256]{2,1,0:T(8,128)(2,1)S(1)}, u32[]{:S(2)}, u32[]{:S(2)}) collective-permute-start(bf16[9,128,256]{2,1,0:T(8,128)(2,1)S(1)} %get-tuple-element.63), channel_id=1, source_target_pairs={{0,2},{2,4},{4,6},{6,8},{8,10},{10,12},{12,14},{14,16},{16,18},{18... | collective-permute-start | bytes 1769480 | tf_op jit(solution)/shard_map/ppermute | solution.py:30
  37.6 4.8 %copy-start = (f32[1,3,3,256,256]{4,3,2,1,0:T(8,128)S(1)}, f32[1,3,3,256,256]{4,3,2,1,0:T(8,128)}, u32[]{:S(2)}) copy-start(f32[1,3,3,256,256]{4,3,2,1,0:T(8,128)} %refs_3_.10) | copy-start | bytes 7077892
  40.5 9.0 %collective-permute-start.7 = (bf16[7,128,256]{2,1,0:T(8,128)(2,1)S(1)}, bf16[7,128,256]{2,1,0:T(8,128)(2,1)S(1)}, u32[]{:S(2)}, u32[]{:S(2)}) collective-permute-start(bf16[7,128,256]{2,1,0:T(8,128)(2,1)S(1)} %get-tuple-element.56.refs_5_), channel_id=1, source_target_pairs={{2,0},{4,2},{6,4},{8,6},{10,8},{12,10},{14,12},{16,14},{18,16},{20... | collective-permute-start | bytes 1376264 | tf_op jit(solution)/shard_map/ppermute | solution.py:30
